TPU v7x, 512 devices: a whole 4x4x16 slice. The times are simulated.
512 devices in a mesh: prow: 16 (over x, y), pcol: 32 (over z, core).
Axes of the slice: x: 4, y: 4, z: 16, core: 2. Of those that a mesh axis runs over, the one named last changes fastest.
Arguments:
- a_matrix: float32 [16384, 8192], P('prow', 'pcol'), as said below
- row_perms: int32 [2, 128], replicated, may hold values from 0 to 127, each once within a row
- dest_rows: int32 [2, 128], replicated, may hold values from 0 to 127, as said below
- row_mask: int32 [2, 128], replicated, may hold values 0 or 1
- col_mask: int32 [2, 64], replicated, may hold values 0 or 1
Outputs:
- schur_out: float32 [16384, 8192], P('prow', 'pcol')
- l_panels: float32 [16384, 256], P('prow')
Inputs may be any that keep to these rules, and one draw needn't show every extreme that they name: `a_matrix`: the two leading diagonal blocks of the window carry 16 sqrt(128) on their diagonal, on top of entries of order one. `dest_rows`: for each section, a permutation of the 128 block rows that keeps a block row's position among the 8 block rows of its device; block rows of one device whose positions differ by less than 16 go to different devices.
All inputs are finite; a program needn't handle non-finite values.
Results may differ from a plain program's by a relative error of at most 0.0001.
Values sent between devices are 32-bit elements; how exact they have to be, the bound alone decides.
No kernel may reach another device: no remote copies, remote signals or barrier semaphores. Data moves between devices by JAX's collectives and lax.ppermute only.
A program may use at most 64 MiB of HBM per device.

v0:
```python
import jax
import jax.numpy as jnp
from jax import lax
from jax.sharding import PartitionSpec as P

SWEEPS = 3


def spread(block, axis, owner):
    block = jnp.where(lax.axis_index(axis) == owner, block, jnp.zeros_like(block))
    return lax.psum(block, axis)


def refine(pivot_block):
    width = pivot_block.shape[0]
    identity = jnp.eye(width, dtype=pivot_block.dtype)
    scale = width * (jnp.mean(pivot_block * pivot_block) + 1e-06)
    approx = pivot_block.T / scale
    for sweep in range(SWEEPS):
        inner = jnp.dot(pivot_block, approx, precision=lax.Precision.HIGHEST)
        approx = jnp.dot(approx, 2.0 * identity - inner, precision=lax.Precision.HIGHEST)
    return approx


def block_flags(mask_row, owner, count, section):
    local = lax.dynamic_slice_in_dim(mask_row, owner * count, count)
    global_ids = owner * count + jnp.arange(count, dtype=jnp.int32)
    return ((local == 1) & (global_ids > section)).astype(jnp.float32)


def shards(a_matrix, row_perms, dest_rows, row_mask, col_mask):
    width = row_perms.shape[1]
    rows_here = a_matrix.shape[0] // width
    cols_here = a_matrix.shape[1] // width
    n_owners = lax.axis_size("prow")
    capacity = (rows_here + n_owners - 1) // n_owners
    my_row = lax.axis_index("prow")
    my_col = lax.axis_index("pcol")
    owner_ids = jnp.arange(n_owners, dtype=jnp.int32)
    slot_ids = jnp.arange(rows_here, dtype=jnp.int32)
    slot_group = slot_ids // n_owners
    group_ids = jnp.arange(capacity, dtype=jnp.int32)
    group_map = (slot_group[:, None] == group_ids[None, :]).astype(jnp.float32)
    current = a_matrix
    panels = []
    for section in range(2):
        root_row = section // rows_here
        local_row = section % rows_here
        local_col = section % cols_here
        block = current[local_row * width : (local_row + 1) * width]
        pivoted = jnp.take(block, row_perms[section], axis=0)
        upper = spread(pivoted, "prow", root_row)
        current = current.at[local_row * width : (local_row + 1) * width].set(
            jnp.where(my_row == root_row, upper, block)
        )
        inverse = refine(upper[:, local_col * width : (local_col + 1) * width])
        column = current[:, local_col * width : (local_col + 1) * width]
        row_flags = block_flags(row_mask[section], my_row, rows_here, section)
        lower = jnp.dot(column, inverse, precision=lax.Precision.HIGHEST)
        lower = lower * jnp.repeat(row_flags, width)[:, None]
        gathered = spread(lower, "pcol", section // cols_here)
        panels.append(gathered)
        col_flags = block_flags(col_mask[section], my_col, cols_here, section)
        kept = upper * jnp.repeat(col_flags, width)[None, :]
        targets = lax.dynamic_slice_in_dim(dest_rows[section], my_row * rows_here, rows_here)
        target_dev = targets // rows_here
        send_map = (
            (target_dev[None, None, :] == owner_ids[:, None, None])
            & (slot_group[None, None, :] == group_ids[None, :, None])
        ).astype(jnp.float32)
        mine = my_row * rows_here + slot_ids
        all_targets = dest_rows[section].reshape(n_owners, rows_here)
        matches = (all_targets[None, :, :] == mine[:, None, None]).astype(jnp.float32)
        recv_map = jnp.einsum("tpr,rk->tpk", matches, group_map, precision=lax.Precision.HIGHEST)
        product = jnp.dot(gathered, kept, precision=lax.Precision.HIGHEST)
        outgoing = jnp.einsum(
            "qkr,rbc->qkbc",
            send_map,
            product.reshape(rows_here, width, -1),
            precision=lax.Precision.HIGHEST,
        ).reshape(n_owners * capacity * width, -1)
        arrived = lax.all_to_all(outgoing, "prow", split_axis=0, concat_axis=0, tiled=True).reshape(
            n_owners, capacity, width, -1
        )
        placed = jnp.einsum(
            "tpk,pkbc->tbc", recv_map, arrived, precision=lax.Precision.HIGHEST
        ).reshape(rows_here * width, -1)
        current = current - placed
    return (current, jnp.concatenate(panels, axis=1))


def solution(mesh):
    placed = (P("prow", "pcol"), P(), P(), P(), P())
    return jax.shard_map(
        shards,
        mesh=mesh,
        in_specs=placed,
        out_specs=(P("prow", "pcol"), P("prow", None)),
        check_vma=False,
    )
```

profile of v0, /device:TPU:8, one launch (start us, length us, event | category | flops | bytes accessed | tf_op | source)
XLA Modules:
  0.0 773.6 jit_solution(13413972947805506345)
XLA Ops:
  7.2 0.0 all-reduce.5.cloned.1.call-start
  7.3 1.2 copy.34
  8.5 0.8 gather_fusion
  9.3 0.7 select_select_fusion.1
  10.0 0.0 all-reduce.5.cloned.1.call-update
  10.1 0.0 all-reduce.7.cloned.1.call-start
  10.1 0.1 fusion.55
  10.2 0.1 broadcast_bitcast_fusion.1
  10.3 0.1 and_select_fusion.1
  10.4 118.5 %all-reduce.5.cloned.1.call-done = f32[128,256]{1,0:T(8,128)} async-done(((f32[128,256]{1,0:T(8,128)}), f32[128,256]{1,0:T(8,128)}) %all-reduce.5.cloned.1.call-update) | async-done | bytes 131088 | tf_op jit(solution)/shard_map/psum | solution.py:11
  128.9 1.5 multiply_reduce_fusion.1
  131.1 1.2 convolution_subtract_fusion.5
  132.3 1.1 fusion.25
  133.4 1.0 convolution_subtract_fusion.4
  134.5 0.2 fusion.77
  134.7 1.0 convolution_subtract_fusion.3
  135.7 0.2 fusion.78
  136.0 1.4 fusion.5
  137.4 0.0 all-reduce.7.cloned.1.call-update
  137.4 0.1 fusion.54
  137.5 0.1 broadcast_bitcast_fusion.3
  137.5 207.9 %all-reduce.7.cloned.1.call-done = f32[1024,128]{1,0:T(8,128)} async-done(((f32[1024,128]{1,0:T(8,128)}), f32[1024,128]{1,0:T(8,128)}) %all-reduce.7.cloned.1.call-update) | async-done | bytes 524304 | tf_op jit(solution)/shard_map/psum | solution.py:11
  345.5 2.0 fusion.14
  347.5 1.5 fusion.8
  349.0 2.5 copy.10
  351.6 7.3 all-to-all-start
  358.8 0.0 all-reduce.9.cloned.1.call-start
  358.9 0.1 eq.155
  359.0 0.1 fusion.53
  359.0 0.2 fusion.20
  359.3 29.3 %all-to-all-done = f32[16,128,256]{2,1,0:T(8,128)S(1)} async-done(((f32[16,128,256]{2,1,0:T(8,128)}), f32[16,128,256]{2,1,0:T(8,128)S(1)}, u32[]{:S(2)}, u32[]{:S(2)}) %all-to-all-start) | async-done | bytes 2097184 | tf_op jit(solution)/shard_map/all_to_all | solution.py:82
  388.5 2.2 fusion.2
  390.8 0.3 copy.12
  391.1 0.1 bitcast_subtract_fusion.1
  391.3 0.8 gather_fusion.1
  392.1 0.7 select_select_fusion
  392.8 0.0 all-reduce.9.cloned.1.call-update
  392.8 0.2 all-reduce.11.cloned.1.call-start
  393.1 0.1 broadcast_bitcast_fusion
  393.1 0.1 fusion.52
  393.2 110.5 %all-reduce.9.cloned.1.call-done = f32[128,256]{1,0:T(8,128)} async-done(((f32[128,256]{1,0:T(8,128)}), f32[128,256]{1,0:T(8,128)}) %all-reduce.9.cloned.1.call-update) | async-done | bytes 131088 | tf_op jit(solution)/shard_map/psum | solution.py:11
  503.7 1.5 multiply_reduce_fusion
  505.9 1.2 convolution_subtract_fusion.2
  507.1 1.1 fusion.22
  508.2 1.0 convolution_subtract_fusion.1
  509.3 0.2 fusion.79
  509.5 1.0 convolution_subtract_fusion
  510.5 0.2 fusion.80
  510.8 1.4 fusion.4
  512.2 0.0 all-reduce.11.cloned.1.call-update
  512.2 0.1 and_select_fusion
  512.3 0.1 broadcast_bitcast_fusion.2
  512.3 207.9 %all-reduce.11.cloned.1.call-done = f32[1024,128]{1,0:T(8,128)} async-done(((f32[1024,128]{1,0:T(8,128)}), f32[1024,128]{1,0:T(8,128)}) %all-reduce.11.cloned.1.call-update) | async-done | bytes 524304 | tf_op jit(solution)/shard_map/psum | solution.py:11
  720.3 2.0 fusion.12
  722.3 1.5 fusion.6
  723.8 2.5 copy.14
  726.4 7.3 all-to-all-start.1
  733.6 0.1 eq.169
  733.7 0.3 fusion.18
  733.9 2.3 pad_maximum_fusion
  736.2 27.2 %all-to-all-done.1 = f32[16,128,256]{2,1,0:T(8,128)S(1)} async-done(((f32[16,128,256]{2,1,0:T(8,128)}), f32[16,128,256]{2,1,0:T(8,128)S(1)}, u32[]{:S(2)}, u32[]{:S(2)}) %all-to-all-start.1) | async-done | bytes 2097184 | tf_op jit(solution)/shard_map/all_to_all | solution.py:82
  763.4 2.2 fusion
  765.6 0.3 copy.16
  766.0 1.1 bitcast_subtract_fusion
  (28 shorter events, 0.2 us)
Async XLA Ops:
  7.2 1.3 copy-start.4
  7.2 3.1 copy-start.5
  7.2 2.9 copy-start.6
  7.2 3.1 copy-start.7
  7.2 121.7 %all-reduce.5.cloned.1.call-start = ((), (), s32[]{:S(2)}) async-start(), calls=%async_computation.2 | async-start | bytes 262144 | tf_op jit(solution)/shard_map/psum | solution.py:11
  10.1 335.4 %all-reduce.7.cloned.1.call-start = ((), (), s32[]{:S(2)}) async-start(), calls=%async_computation.3 | async-start | bytes 1048576 | tf_op jit(solution)/shard_map/psum | solution.py:11
  128.9 216.6 %copy-start.2 = (f32[128,256]{1,0:T(8,128)S(1)}, f32[128,256]{1,0:T(8,128)}, u32[]{:S(2)}) copy-start(f32[128,256]{1,0:T(8,128)} %all-reduce.5.cloned.1.call-done) | copy-start | bytes 393220
  136.0 213.0 %copy-start = (f32[1024,256]{1,0:T(8,128)}, f32[1024,256]{1,0:T(8,128)S(1)}, u32[]{:S(2)}) copy-start(f32[1024,256]{1,0:T(8,128)S(1)} %select_dynamic-update-slice_fusion.1) | copy-start | bytes 3145732
  351.6 37.0 %all-to-all-start = ((f32[16,128,256]{2,1,0:T(8,128)}), f32[16,128,256]{2,1,0:T(8,128)S(1)}, u32[]{:S(2)}, u32[]{:S(2)}) async-start(f32[16,128,256]{2,1,0:T(8,128)} %copy.10), calls=%async_computation | async-start | bytes 4194304 | tf_op jit(solution)/shard_map/all_to_all | solution.py:82
  358.8 144.9 %all-reduce.9.cloned.1.call-start = ((), (), s32[]{:S(2)}) async-start(), calls=%async_computation.4 | async-start | bytes 262144 | tf_op jit(solution)/shard_map/psum | solution.py:11
  388.5 2.6 copy-start.1
  392.8 327.4 %all-reduce.11.cloned.1.call-start = ((), (), s32[]{:S(2)}) async-start(), calls=%async_computation.5 | async-start | bytes 1048576 | tf_op jit(solution)/shard_map/psum | solution.py:11
  503.7 216.6 %copy-start.3 = (f32[128,256]{1,0:T(8,128)S(1)}, f32[128,256]{1,0:T(8,128)}, u32[]{:S(2)}) copy-start(f32[128,256]{1,0:T(8,128)} %all-reduce.9.cloned.1.call-done) | copy-start | bytes 393220
  726.4 37.0 %all-to-all-start.1 = ((f32[16,128,256]{2,1,0:T(8,128)}), f32[16,128,256]{2,1,0:T(8,128)S(1)}, u32[]{:S(2)}, u32[]{:S(2)}) async-start(f32[16,128,256]{2,1,0:T(8,128)} %copy.14), calls=%async_computation.1 | async-start | bytes 4194304 | tf_op jit(solution)/shard_map/all_to_all | solution.py:82
Sparse Core Ops, SparseCore 0:
  11.8 117.0 all-reduce.4
  137.5 207.9 all-reduce.6
  393.0 110.6 all-reduce.8
  512.3 207.9 all-reduce.10
where the time goes:
time: 774 us
  waiting for transfers between devices  701 us (91%)
  matrix products  24.4 us (3%)
  between operations  15.4 us (2%)
  starting transfers between devices  14.8 us (2%)
  local copies, waits for them, and re-layouts  9.03 us (1%)
  other arithmetic  8.62 us (1%)
    psum x4, waiting for transfers between devices, spread(): return lax.psum(block, axis)  645 us
    all_to_all x2, waiting for transfers between devices, shards(): lax.all_to_all(outgoing, 'prow', split_axis=0, concat_axis=0, tiled=True)  56.4 us
  transfers between devices with their start and end apart: 6, of which 6 were waited for; matrix products, arithmetic and copies ran while one was open for 0% of the time, Pallas kernels for 0%

commit v1 on v0

--- a/solution.py
+++ b/solution.py
@@ -8,7 +8,7 @@
 
 def spread(block, axis, owner):
     block = jnp.where(lax.axis_index(axis) == owner, block, jnp.zeros_like(block))
-    return lax.psum(block, axis)
+    return jnp.sum(lax.all_gather(block, axis), axis=0)
 
 
 def refine(pivot_block):

time: 774 us -> 469 us (0.61)
  waiting for transfers between devices: 701 us -> 391 us
  other arithmetic: 8.62 us -> 23.3 us
  matrix products: 24.4 us -> 14.9 us
    psum x4 -> x0, waiting for transfers between devices: 645 us -> none  [spread(): return lax.psum(block, axis)]
    all_gather x0 -> x4, waiting for transfers between devices: none -> 335 us  [spread(): return jnp.sum(lax.all_gather(block, axis), axis=0)]
    reduce_sum x0 -> x4, other arithmetic: none -> 16.6 us  [spread(): return jnp.sum(lax.all_gather(block, axis), axis=0)]
  transfers between devices with their start and end apart: 6 -> 6, of which waited for: 6 -> 6; matrix products, arithmetic and copies ran while one was open for 0% -> 1% of each run, Pallas kernels for 0% -> 0%
where the time goes in v1:
time: 469 us
  waiting for transfers between devices  391 us (83%)
  other arithmetic  23.3 us (5%)
  between operations  15.4 us (3%)
  matrix products  14.9 us (3%)
  starting transfers between devices  14.8 us (3%)
  local copies, waits for them, and re-layouts  9.07 us (2%)
    all_gather x4, waiting for transfers between devices, spread(): return jnp.sum(lax.all_gather(block, axis), axis=0)  335 us
    all_to_all x2, waiting for transfers between devices, shards(): lax.all_to_all(outgoing, 'prow', split_axis=0, concat_axis=0, tiled=True)  56.7 us
    reduce_sum x4, other arithmetic, spread(): return jnp.sum(lax.all_gather(block, axis), axis=0)  16.6 us
    all_to_all x2, starting transfers between devices, shards(): lax.all_to_all(outgoing, 'prow', split_axis=0, concat_axis=0, tiled=True)  14.5 us
  transfers between devices with their start and end apart: 6, of which 6 were waited for; matrix products, arithmetic and copies ran while one was open for 1% of the time, Pallas kernels for 0%

profile of v1, /device:TPU:8, one launch (start us, length us, event | category | flops | bytes accessed | tf_op | source)
XLA Modules:
  0.0 468.9 jit_solution(471122554007233472)
XLA Ops:
  7.2 0.0 all-gather.9.cloned.1.call-start
  7.2 1.2 copy.34
  8.5 0.8 gather_fusion
  9.3 0.7 select_select_fusion.1
  10.0 0.0 all-gather.9.cloned.1.call-update
  10.0 0.0 all-gather.11.cloned.1.call-start
  10.1 0.1 fusion.57
  10.2 0.1 broadcast_bitcast_fusion.1
  10.3 65.7 %all-gather.9.cloned.1.call-done = f32[2048,256]{1,0:T(8,128)} async-done(((f32[128,256]{1,0:T(8,128)}), f32[2048,256]{1,0:T(8,128)}) %all-gather.9.cloned.1.call-update) | async-done | bytes 2097168 | tf_op jit(solution)/shard_map/all_gather | solution.py:11
  75.9 1.7 reduce_sum.54
  77.7 0.6 multiply_reduce_fusion.1
  79.0 0.3 convolution_subtract_fusion.5
  79.3 0.3 fusion.25
  79.6 0.2 convolution_subtract_fusion.4
  79.8 0.2 fusion.79
  80.0 0.2 convolution_subtract_fusion.3
  80.2 0.2 fusion.80
  80.4 1.4 fusion.5
  81.8 0.1 fusion.56
  81.9 0.1 and_select_fusion
  82.0 0.1 broadcast_bitcast_fusion.3
  82.1 106.5 %all-gather.11.cloned.1.call-done = f32[32768,128]{1,0:T(8,128)} async-done(((f32[1024,128]{1,0:T(8,128)}), f32[32768,128]{1,0:T(8,128)}) %all-gather.11.cloned.1.call-update) | async-done | bytes 16777232 | tf_op jit(solution)/shard_map/all_gather | solution.py:11
  188.5 6.6 %reduce_sum.56 = f32[1024,128]{1,0:T(8,128)S(1)} reduce(f32[32,1024,128]{2,1,0:T(8,128)} %bitcast.92, f32[]{:T(128)} %constant.132.clone.1), dimensions={0}, to_apply=%region_2.4 | reduce | flops 4063232 | bytes 17301508 | tf_op jit(solution)/shard_map/reduce_sum | solution.py:11
  195.1 1.1 fusion.10
  196.2 1.1 fusion.46
  197.4 2.6 copy.10
  199.9 7.3 %all-to-all-start = ((f32[16,128,256]{2,1,0:T(8,128)}), f32[16,128,256]{2,1,0:T(8,128)S(1)}, u32[]{:S(2)}, u32[]{:S(2)}) async-start(f32[16,128,256]{2,1,0:T(8,128)} %copy.10), calls=%async_computation | async-start | bytes 4194304 | tf_op jit(solution)/shard_map/all_to_all | solution.py:82
  207.2 0.0 all-gather.13.cloned.1.call-start
  207.2 0.1 eq.129
  207.3 0.2 fusion.20
  207.6 29.5 %all-to-all-done = f32[16,128,256]{2,1,0:T(8,128)S(1)} async-done(((f32[16,128,256]{2,1,0:T(8,128)}), f32[16,128,256]{2,1,0:T(8,128)S(1)}, u32[]{:S(2)}, u32[]{:S(2)}) %all-to-all-start) | async-done | bytes 2097184 | tf_op jit(solution)/shard_map/all_to_all | solution.py:82
  237.0 2.2 fusion.2
  239.3 0.3 copy.12
  239.6 0.1 bitcast_subtract_fusion.1
  239.8 0.8 gather_fusion.1
  240.6 0.7 select_select_fusion
  241.3 0.2 all-gather.15.cloned.1.call-start
  241.6 0.1 fusion.55
  241.6 0.1 broadcast_bitcast_fusion
  241.7 55.9 %all-gather.13.cloned.1.call-done = f32[2048,256]{1,0:T(8,128)} async-done(((f32[128,256]{1,0:T(8,128)}), f32[2048,256]{1,0:T(8,128)}) %all-gather.13.cloned.1.call-update) | async-done | bytes 2097168 | tf_op jit(solution)/shard_map/all_gather | solution.py:11
  297.6 1.7 reduce_sum.57
  299.3 0.6 multiply_reduce_fusion
  300.6 0.3 convolution_subtract_fusion.2
  300.9 0.3 fusion.22
  301.2 0.2 convolution_subtract_fusion.1
  301.4 0.2 fusion.81
  301.6 0.2 convolution_subtract_fusion
  301.8 0.2 fusion.82
  302.0 1.4 fusion.4
  303.4 0.1 fusion.54
  303.5 0.1 broadcast_bitcast_fusion.2
  303.6 106.6 %all-gather.15.cloned.1.call-done = f32[32768,128]{1,0:T(8,128)} async-done(((f32[1024,128]{1,0:T(8,128)}), f32[32768,128]{1,0:T(8,128)}) %all-gather.15.cloned.1.call-update) | async-done | bytes 16777232 | tf_op jit(solution)/shard_map/all_gather | solution.py:11
  410.1 6.6 %reduce_sum.59 = f32[1024,128]{1,0:T(8,128)S(1)} reduce(f32[32,1024,128]{2,1,0:T(8,128)} %bitcast.93, f32[]{:T(128)} %constant.132.clone.1), dimensions={0}, to_apply=%region_5.7 | reduce | flops 4063232 | bytes 17301508 | tf_op jit(solution)/shard_map/reduce_sum | solution.py:11
  416.7 1.1 fusion.8
  417.8 1.1 fusion.50
  419.0 2.6 copy.14
  421.5 7.3 %all-to-all-start.1 = ((f32[16,128,256]{2,1,0:T(8,128)}), f32[16,128,256]{2,1,0:T(8,128)S(1)}, u32[]{:S(2)}, u32[]{:S(2)}) async-start(f32[16,128,256]{2,1,0:T(8,128)} %copy.14), calls=%async_computation.1 | async-start | bytes 4194304 | tf_op jit(solution)/shard_map/all_to_all | solution.py:82
  428.8 0.1 eq.143
  428.9 0.3 fusion.18
  429.1 2.3 pad_maximum_fusion
  431.4 27.3 %all-to-all-done.1 = f32[16,128,256]{2,1,0:T(8,128)S(1)} async-done(((f32[16,128,256]{2,1,0:T(8,128)}), f32[16,128,256]{2,1,0:T(8,128)S(1)}, u32[]{:S(2)}, u32[]{:S(2)}) %all-to-all-start.1) | async-done | bytes 2097184 | tf_op jit(solution)/shard_map/all_to_all | solution.py:82
  458.6 2.2 fusion
  460.9 0.3 copy.16
  461.2 1.1 bitcast_subtract_fusion
  (31 shorter events, 0.2 us)
Async XLA Ops:
  7.2 1.3 copy-start.4
  7.2 2.9 copy-start.6
  7.2 68.7 %all-gather.9.cloned.1.call-start = ((), (), s32[]{:S(2)}) async-start(), calls=%async_computation.2 | async-start | bytes 2228224 | tf_op jit(solution)/shard_map/all_gather | solution.py:11
  10.0 178.5 %all-gather.11.cloned.1.call-start = ((), (), s32[]{:S(2)}) async-start(), calls=%async_computation.3 | async-start | bytes 17301504 | tf_op jit(solution)/shard_map/all_gather | solution.py:11
  77.7 4.2 copy-start.7
  77.7 4.3 copy-start.5
  78.3 116.8 %copy-start = (f32[1024,256]{1,0:T(8,128)}, f32[1024,256]{1,0:T(8,128)S(1)}, u32[]{:S(2)}) copy-start(f32[1024,256]{1,0:T(8,128)S(1)} %select_dynamic-update-slice_fusion.1) | copy-start | bytes 3145732
  195.1 2.2 copy-start.2
  199.9 37.1 %all-to-all-start = ((f32[16,128,256]{2,1,0:T(8,128)}), f32[16,128,256]{2,1,0:T(8,128)S(1)}, u32[]{:S(2)}, u32[]{:S(2)}) async-start(f32[16,128,256]{2,1,0:T(8,128)} %copy.10), calls=%async_computation | async-start | bytes 4194304 | tf_op jit(solution)/shard_map/all_to_all | solution.py:82
  207.2 90.4 %all-gather.13.cloned.1.call-start = ((), (), s32[]{:S(2)}) async-start(), calls=%async_computation.4 | async-start | bytes 2228224 | tf_op jit(solution)/shard_map/all_gather | solution.py:11
  237.0 2.6 copy-start.1
  241.3 168.8 %all-gather.15.cloned.1.call-start = ((), (), s32[]{:S(2)}) async-start(), calls=%async_computation.5 | async-start | bytes 17301504 | tf_op jit(solution)/shard_map/all_gather | solution.py:11
  416.7 2.2 copy-start.3
  421.5 37.1 %all-to-all-start.1 = ((f32[16,128,256]{2,1,0:T(8,128)}), f32[16,128,256]{2,1,0:T(8,128)S(1)}, u32[]{:S(2)}, u32[]{:S(2)}) async-start(f32[16,128,256]{2,1,0:T(8,128)} %copy.14), calls=%async_computation.1 | async-start | bytes 4194304 | tf_op jit(solution)/shard_map/all_to_all | solution.py:82
Sparse Core Ops, SparseCore 0:
  11.6 64.2 all-gather.8
  81.9 106.5 all-gather.10
  241.5 56.0 all-gather.12
  303.5 106.5 all-gather.14
